TPU v7x, 32 devices: a whole 2x2x4 slice. The times are simulated.
32 devices in a mesh: stream: 8 (over y, x, core), cross: 4 (over z).
Axes of the slice: x: 2, y: 2, z: 4, core: 2. Of those that a mesh axis runs over, the one named last changes fastest.
Arguments:
- initial_state: float32 [5, 64, 32768], P(None, 'stream', 'cross'), may hold values from -6 to 6
- forcing: float32 [5, 64, 32768], P(None, 'stream', 'cross'), may hold values from -0.3 to 0.3
- block_inverse: float32 [5, 5, 64, 32768], P(None, None, 'stream', 'cross'), may hold values from -1 to 1, as said below
- lower_decay: float32 [5, 64, 32768], P(None, 'stream', 'cross'), may hold values from 0 to 1
- upper_decay: float32 [5, 64, 32768], P(None, 'stream', 'cross'), may hold values from 0 to 1
- cross_coupling: float32 [64, 32768], P('stream', 'cross'), may hold values from 0.002 to 0.02
- iblank: int32 [64, 32768], P('stream', 'cross'), may hold values 0 or 1
- donor_receiver: int32 [1024, 1], P(('stream', 'cross')), may hold values from 0 to 31; in each aligned block of 32 rows (0 to 31, 32 to 63, ...) at most 2 rows name the same one
- donor_block: int32 [1024], P(('stream', 'cross')), may hold values from 0 to 511
- stencil_offset: int32 [1024], P(('stream', 'cross')), may hold values from 1 to 127
- stencil_weight: float32 [1024, 128], P(('stream', 'cross')), may hold values from 0.005 to 0.02
- fringe_target: int32 [2048], P(('stream', 'cross')), may hold values from 0 to 511
Outputs:
- final_state: float32 [5, 64, 32768], P(None, 'stream', 'cross')
- last_update: float32 [5, 64, 32768], P(None, 'stream', 'cross')
Inputs may be any that keep to these rules, and one draw needn't show every extreme that they name: `donor_receiver`: within the rows of one device no receiving device is named more than 2 times. `block_inverse`: each 5 x 5 block is orthogonal and symmetric.
All inputs are finite; a program needn't handle non-finite values. No bound on the sum of `iblank` on one device may be relied on, other than what follows from the above.
Results may differ from a plain program's by a relative error of at most 0.00018.
Values sent between devices are 32-bit elements; how exact they have to be, the bound alone decides.
A program may use at most 128 MiB of HBM per device.

v0:
```python
import jax
import jax.numpy as jnp
from jax import lax
from jax.sharding import PartitionSpec as P

ITERS = 2
CAP = 2


def padded_2(cells, sides, width):
    for axis, dim in sides:
        count = lax.axis_size(axis)
        head = lax.slice_in_dim(cells, 0, width, axis=dim)
        tail = lax.slice_in_dim(cells, cells.shape[dim] - width, cells.shape[dim], axis=dim)
        cells = jnp.concatenate(
            [
                lax.ppermute(tail, axis, [(i, (i + 1) % count) for i in range(count)]),
                cells,
                lax.ppermute(head, axis, [((i + 1) % count, i) for i in range(count)]),
            ],
            axis=dim,
        )
    return cells


def passed_along(value, axis, steps):
    count = lax.axis_size(axis)
    initial, last = (max(0, -steps), min(count, count - steps))
    return lax.ppermute(value, axis, [(source, source + steps) for source in range(initial, last)])


def apply_block(block_inv, vector):
    return jnp.sum(block_inv * vector[None], axis=1)


def multiply_maps(left, right):
    return jnp.sum(left[:, :, None, :] * right[None], axis=1)


def plane_of(array, index, axis):
    return lax.dynamic_index_in_dim(array, index, axis, keepdims=False)


def compose_down(driving_term, block_inv, decay):
    count = driving_term.shape[1]
    cells = driving_term.shape[2]
    identity = jnp.broadcast_to(jnp.eye(5, dtype=jnp.float32)[:, :, None], (5, 5, cells))

    def step(index, carry):
        matrix, offset = carry
        inverse = plane_of(block_inv, index, 2)
        factor = plane_of(decay, index, 1)
        matrix = multiply_maps(inverse, factor[:, None, :] * matrix)
        offset = apply_block(inverse, plane_of(driving_term, index, 1) + factor * offset)
        return (matrix, offset)

    return lax.fori_loop(0, count, step, (identity, jnp.zeros((5, cells), jnp.float32)))


def compose_up(near, block_inv, decay):
    count = near.shape[1]
    cells = near.shape[2]
    identity = jnp.broadcast_to(jnp.eye(5, dtype=jnp.float32)[:, :, None], (5, 5, cells))

    def step(turn, carry):
        matrix, offset = carry
        index = count - 1 - turn
        inverse = plane_of(block_inv, index, 2)
        factor = plane_of(decay, index, 1)
        matrix = multiply_maps(inverse, factor[:, None, :] * matrix)
        offset = plane_of(near, index, 1) + apply_block(inverse, factor * offset)
        return (matrix, offset)

    return lax.fori_loop(0, count, step, (identity, jnp.zeros((5, cells), jnp.float32)))


def sweep_down(driving_term, block_inv, decay, incoming):
    count = driving_term.shape[1]

    def step(index, carry):
        face, sweep_output = carry
        face = apply_block(
            plane_of(block_inv, index, 2),
            plane_of(driving_term, index, 1) + plane_of(decay, index, 1) * face,
        )
        return (face, lax.dynamic_update_index_in_dim(sweep_output, face, index, 1))

    return lax.fori_loop(0, count, step, (incoming, jnp.zeros_like(driving_term)))[1]


def sweep_up(near, block_inv, decay, incoming):
    count = near.shape[1]

    def step(turn, carry):
        face, sweep_output = carry
        index = count - 1 - turn
        face = plane_of(near, index, 1) + apply_block(
            plane_of(block_inv, index, 2), plane_of(decay, index, 1) * face
        )
        return (face, lax.dynamic_update_index_in_dim(sweep_output, face, index, 1))

    return lax.fori_loop(0, count, step, (incoming, jnp.zeros_like(near)))[1]


def shards(
    initial_state,
    forcing,
    block_inverse,
    lower_decay,
    upper_decay,
    cross_coupling,
    iblank,
    donor_receiver,
    donor_block,
    stencil_offset,
    stencil_weight,
    fringe_target,
):
    stream_count = lax.axis_size("stream")
    cross_count = lax.axis_size("cross")
    devices = stream_count * cross_count
    planes = initial_state.shape[1]
    cells = initial_state.shape[2]
    block_count = planes * cells // 128
    senders = donor_block.shape[0]
    hole = (1 - iblank).astype(jnp.float32)
    receiver = donor_receiver[:, 0]
    order = lax.broadcasted_iota(jnp.int32, (senders, senders), 1)
    earlier = order < order.T
    same = receiver[:, None] == receiver[None, :]
    slot_rank = jnp.sum((same & earlier).astype(jnp.int32), axis=1)
    destination = receiver * CAP + slot_rank
    block_ids = lax.broadcasted_iota(jnp.int32, (senders, block_count), 1)
    pick_table = (donor_block[:, None] == block_ids).astype(jnp.float32)
    source_lane = lax.broadcasted_iota(jnp.int32, (senders, 128, 128), 1)
    target_lane = lax.broadcasted_iota(jnp.int32, (senders, 128, 128), 2)
    offset_lookup = (source_lane == (target_lane + stencil_offset[:, None, None]) % 128).astype(
        jnp.float32
    )
    slot_ids = lax.broadcasted_iota(jnp.int32, (devices * CAP, senders), 0)
    place_table = (destination[None, :] == slot_ids).astype(jnp.float32)
    column_entries = lax.broadcasted_iota(jnp.int32, (block_count, devices * CAP), 0)
    onehot = (fringe_target[None, :] == column_entries).astype(jnp.float32)
    blank_face = jnp.zeros((5, cells), jnp.float32)
    state = initial_state
    update = jnp.zeros_like(initial_state)
    for relaxation_round in range(ITERS):
        padded = padded_2(state, (("cross", 2),), 1)
        laplace = 2.0 * state - padded[:, :, :-2] - padded[:, :, 2:]
        blocks_local = state.reshape(5, block_count, 128)
        selected_values = jnp.einsum(
            "eb,vbp->vep", pick_table, blocks_local, precision=lax.Precision.HIGHEST
        )
        displaced_values = jnp.einsum(
            "mub,ubh->muh", selected_values, offset_lookup, precision=lax.Precision.HIGHEST
        )
        values = stencil_weight[None] * (selected_values + displaced_values)
        outgoing = jnp.einsum("se,vep->vsp", place_table, values, precision=lax.Precision.HIGHEST)
        received = lax.all_to_all(
            outgoing, ("stream", "cross"), split_axis=1, concat_axis=1, tiled=True
        )
        fringe = jnp.einsum(
            "bs,vsp->vbp", onehot, received, precision=lax.Precision.HIGHEST
        ).reshape(state.shape)
        driving_term = forcing - cross_coupling[None] * laplace + hole[None] * fringe
        matrix_down, offset_down = compose_down(driving_term, block_inverse, lower_decay)

        def pass_down(turn, carry):
            face, incoming = carry
            incoming = passed_along(face, "stream", 1)
            return (apply_block(matrix_down, incoming) + offset_down, incoming)

        incoming_down = lax.fori_loop(0, stream_count, pass_down, (offset_down, blank_face))[1]
        near = sweep_down(driving_term, block_inverse, lower_decay, incoming_down)
        matrix_up, offset_up = compose_up(near, block_inverse, upper_decay)

        def pass_up(turn, carry):
            face, incoming = carry
            incoming = passed_along(face, "stream", -1)
            return (apply_block(matrix_up, incoming) + offset_up, incoming)

        incoming_up = lax.fori_loop(0, stream_count, pass_up, (offset_up, blank_face))[1]
        update = sweep_up(near, block_inverse, upper_decay, incoming_up)
        state = state + update
    return (state, update)


def solution(mesh):
    return jax.shard_map(
        shards,
        mesh=mesh,
        in_specs=(
            P(None, "stream", "cross"),
            P(None, "stream", "cross"),
            P(None, None, "stream", "cross"),
            P(None, "stream", "cross"),
            P(None, "stream", "cross"),
            P("stream", "cross"),
            P("stream", "cross"),
            P(("stream", "cross"), None),
            P(("stream", "cross")),
            P(("stream", "cross")),
            P(("stream", "cross"), None),
            P(("stream", "cross")),
        ),
        out_specs=(P(None, "stream", "cross"), P(None, "stream", "cross")),
        check_vma=False,
    )
```

profile of v0, /device:TPU:3, one launch (start us, length us, event | category | flops | bytes accessed | tf_op | source)
XLA Modules:
  0.0 806.4 jit_solution(11326317212507014265)
XLA Ops:
  5.4 6.5 all-to-all-start
  15.9 11.0 %copy.72 = f32[5,5,8,8192]{3,1,0,2:T(8,128)} copy(f32[5,5,8,8192]{3,2,1,0:T(8,128)} %param.38) | data formatting | bytes 13107200
  44.0 36.2 %while.178 = (s32[]{:T(128)}, f32[5,5,8192]{2,1,0:T(8,128)S(1)}, f32[5,8192]{1,0:T(8,128)}, f32[5,5,8,8192]{3,1,0,2:T(8,128)}, f32[5,8,8192]{2,0,1:T(8,128)S(1)}, /*index=5*/f32[5,8,8192]{2,0,1:T(8,128)}, s32[]{:T(128)}) while((s32[]{:T(128)}, f32[5,5,8192]{2,1,0:T(8,128)S(1)}, f32[5,8192]{1,0:T(8,128)}, f32[5,5,8,8192]{3,1,0,2:T(8,128)}, ...), condition=%wide.region_4.5_spmd, body=%wide.region_1.4_spmd.sunk | while | flops 2498562 | bytes 7209049 | solution.py:57
  82.8 79.5 %while.179 = (s32[]{:T(128)}, f32[5,8192]{1,0:T(8,128)}, f32[5,8192]{1,0:T(8,128)}, f32[5,5,8192]{2,1,0:T(8,128)S(1)}, f32[5,8192]{1,0:T(8,128)}, /*index=5*/s32[]{:T(128)}) while((s32[]{:T(128)}, f32[5,8192]{1,0:T(8,128)}, f32[5,8192]{1,0:T(8,128)}, f32[5,5,8192]{2,1,0:T(8,128)S(1)}, f32[5,8192]{1,0:T(8,128)}, /*index=5*/s32[]{:T(128)}) %tuple.350), condition=%wide.region_7.8_spmd, body=%wide.region_5.7_spmd.sunk | while | flops 409602 | bytes 3604645 | solution.py:173
  82.8 4.0 collective-permute-start
  91.6 5.3 collective-permute-start
  101.7 5.3 collective-permute-start
  111.8 5.3 collective-permute-start
  121.9 5.3 collective-permute-start
  132.0 5.3 collective-permute-start
  142.1 5.3 collective-permute-start
  152.2 5.3 collective-permute-start
  163.3 54.0 %while.180 = (s32[]{:T(128)}, f32[5,8192]{1,0:T(8,128)S(1)}, f32[5,8,8192]{2,1,0:T(8,128)S(1)}, f32[5,5,8,8192]{3,2,1,0:T(8,128)}, f32[5,8,8192]{2,0,1:T(8,128)}...) while((s32[]{:T(128)}, f32[5,8192]{1,0:T(8,128)S(1)}, f32[5,8,8192]{2,1,0:T(8,128)S(1)}, ...), condition=%wide.region_10.11_spmd, body=%wide.region_8.10_spmd.sunk | while | flops 450562 | bytes 4096097 | solution.py:88
  164.4 3.6 constant_dynamic-slice_fusion.16
  171.1 3.6 constant_dynamic-slice_fusion.16
  177.9 3.6 constant_dynamic-slice_fusion.16
  184.6 3.6 constant_dynamic-slice_fusion.16
  198.1 3.6 constant_dynamic-slice_fusion.16
  204.9 3.6 constant_dynamic-slice_fusion.16
  211.6 3.6 constant_dynamic-slice_fusion.16
  218.2 31.9 %while.188 = (s32[]{:T(128)}, f32[5,5,8192]{2,1,0:T(8,128)S(1)}, f32[5,8192]{1,0:T(8,128)S(1)}, f32[5,5,8,8192]{3,1,0,2:T(8,128)}, f32[5,8,8192]{2,0,1:T(8,128)}...) while((s32[]{:T(128)}, f32[5,5,8192]{2,1,0:T(8,128)S(1)}, ...), condition=%wide.region_14.15_spmd.clone, body=%wide.region_11.14_spmd.clone.sunk | while | flops 2539527 | bytes 7700649 | solution.py:74
  251.5 80.3 %while.181 = (s32[]{:T(128)}, f32[5,8192]{1,0:T(8,128)}, f32[5,8192]{1,0:T(8,128)}, f32[5,5,8192]{2,1,0:T(8,128)S(1)}, f32[5,8192]{1,0:T(8,128)S(1)}, /*index=5*/s32[]{:T(128)}) while((s32[]{:T(128)}, f32[5,8192]{1,0:T(8,128)}, f32[5,8192]{1,0:T(8,128)}, f32[5,5,8192]{2,1,0:T(8,128)S(1)}, f32[5,8192]{1,0:T(8,128)S(1)}, ...), condition=%wide.region_17.18_spmd, body=%wide.region_15.17_spmd.sunk | while | flops 409602 | bytes 2949257 | solution.py:182
  253.5 7.5 collective-permute-done.1
  264.1 6.9 collective-permute-done.1
  274.0 6.9 collective-permute-done.1
  284.0 6.9 collective-permute-done.1
  293.9 6.9 collective-permute-done.1
  303.9 6.9 collective-permute-done.1
  313.8 6.9 collective-permute-done.1
  323.8 6.9 collective-permute-done.1
  333.0 82.2 %while.182 = (s32[]{:T(128)}, f32[5,8192]{1,0:T(8,128)S(1)}, f32[5,8,8192]{2,1,0:T(8,128)}, f32[5,8,8192]{2,1,0:T(8,128)S(1)}, f32[5,5,8,8192]{3,2,1,0:T(8,128)}...) while((s32[]{:T(128)}, f32[5,8192]{1,0:T(8,128)S(1)}, ...), condition=%wide.region_20.21_spmd, body=%wide.region_18.20_spmd.sunk | while | flops 491526 | bytes 4751523 | solution.py:102
  333.0 3.7 constant_dynamic-slice_fusion.17
  339.0 4.2 dynamic_update_slice.41
  349.3 4.2 dynamic_update_slice.41
  359.5 4.2 dynamic_update_slice.41
  369.8 4.2 dynamic_update_slice.41
  380.0 4.2 dynamic_update_slice.41
  390.3 4.2 dynamic_update_slice.41
  400.6 4.2 dynamic_update_slice.41
  410.8 4.2 dynamic_update_slice.41
  426.0 6.9 all-to-all-done.1
  441.1 38.1 %while.183 = (s32[]{:T(128)}, f32[5,5,8192]{2,1,0:T(8,128)S(1)}, f32[5,8192]{1,0:T(8,128)S(1)}, f32[5,5,8,8192]{3,1,0,2:T(8,128)}, f32[5,8,8192]{2,0,1:T(8,128)}, /*index=5*/f32[5,8,8192]{2,0,1:T(8,128)}, s32[]{:T(128)}) while((s32[]{:T(128)}, f32[5,5,8192]{2,1,0:T(8,128)S(1)}, f32[5,8192]{1,0:T(8,128)S(1)}, f32[5,5,8,8192]{3,1,0,2:T(8,128)}, ...), condition=%wide.region_24.25_spmd, body=%wide.region_21.24_spmd.sunk | while | flops 2498562 | bytes 7209049 | solution.py:57
  480.6 77.4 %while.184 = (s32[]{:T(128)}, f32[5,8192]{1,0:T(8,128)}, f32[5,8192]{1,0:T(8,128)}, f32[5,5,8192]{2,1,0:T(8,128)S(1)}, f32[5,8192]{1,0:T(8,128)S(1)}, /*index=5*/s32[]{:T(128)}) while((s32[]{:T(128)}, f32[5,8192]{1,0:T(8,128)}, f32[5,8192]{1,0:T(8,128)}, f32[5,5,8192]{2,1,0:T(8,128)S(1)}, f32[5,8192]{1,0:T(8,128)S(1)}, ...), condition=%wide.region_27.28_spmd, body=%wide.region_25.27_spmd.sunk | while | flops 409602 | bytes 2949257 | solution.py:173
  488.3 5.2 collective-permute-start.2
  498.3 5.2 collective-permute-start.2
  508.2 5.2 collective-permute-start.2
  518.2 5.2 collective-permute-start.2
  528.1 5.2 collective-permute-start.2
  538.1 5.2 collective-permute-start.2
  548.1 5.2 collective-permute-start.2
  559.0 54.0 %while.185 = (s32[]{:T(128)}, f32[5,8192]{1,0:T(8,128)S(1)}, f32[5,8,8192]{2,1,0:T(8,128)S(1)}, f32[5,5,8,8192]{3,2,1,0:T(8,128)}, f32[5,8,8192]{2,0,1:T(8,128)}...) while((s32[]{:T(128)}, f32[5,8192]{1,0:T(8,128)S(1)}, f32[5,8,8192]{2,1,0:T(8,128)S(1)}, ...), condition=%wide.region_30.31_spmd, body=%wide.region_28.30_spmd.sunk | while | flops 450562 | bytes 4096097 | solution.py:88
  560.0 3.6 constant_dynamic-slice_fusion.18
  566.8 3.6 constant_dynamic-slice_fusion.18
  614.2 42.2 %while.189 = (s32[]{:T(128)}, f32[5,5,8192]{2,1,0:T(8,128)S(1)}, f32[5,8192]{1,0:T(8,128)S(1)}, f32[5,5,8,8192]{3,1,0,2:T(8,128)}, f32[5,8,8192]{2,0,1:T(8,128)}...) while((s32[]{:T(128)}, f32[5,5,8192]{2,1,0:T(8,128)S(1)}, ...), condition=%wide.region_34.35_spmd.clone, body=%wide.region_31.34_spmd.clone.sunk | while | flops 2539527 | bytes 7700649 | solution.py:74
  657.8 80.3 %while.186 = (s32[]{:T(128)}, f32[5,8192]{1,0:T(8,128)}, f32[5,8192]{1,0:T(8,128)}, f32[5,5,8192]{2,1,0:T(8,128)S(1)}, f32[5,8192]{1,0:T(8,128)S(1)}, /*index=5*/s32[]{:T(128)}) while((s32[]{:T(128)}, f32[5,8192]{1,0:T(8,128)}, f32[5,8192]{1,0:T(8,128)}, f32[5,5,8192]{2,1,0:T(8,128)S(1)}, f32[5,8192]{1,0:T(8,128)S(1)}, ...), condition=%wide.region_37.38_spmd, body=%wide.region_35.37_spmd.sunk | while | flops 409602 | bytes 2949257 | solution.py:182
  659.7 7.5 collective-permute-done.3
  670.3 6.9 collective-permute-done.3
  680.3 6.9 collective-permute-done.3
  690.2 6.9 collective-permute-done.3
  700.2 6.9 collective-permute-done.3
  710.1 6.9 collective-permute-done.3
  720.1 6.9 collective-permute-done.3
  730.0 6.9 collective-permute-done.3
  739.0 65.9 %while.187 = (s32[]{:T(128)}, f32[5,8192]{1,0:T(8,128)S(1)}, f32[5,8,8192]{2,1,0:T(8,128)S(1)}, f32[5,8,8192]{2,1,0:T(8,128)}, f32[5,5,8,8192]{3,2,1,0:T(8,128)}...) while((s32[]{:T(128)}, f32[5,8192]{1,0:T(8,128)S(1)}, ...), condition=%wide.region_40.41_spmd, body=%wide.region_38.40_spmd.sunk | while | flops 491526 | bytes 4751523 | solution.py:102
  (579 shorter events, 519.0 us)
Async XLA Ops:
  0.6 1.5 copy-start.23
  0.6 1.7 copy-start.21
  3.0 1.2 copy-start.20
  3.0 8.9 %copy-start.11 = (f32[5,8,8192]{2,1,0:T(8,128)S(1)}, f32[5,8,8192]{2,1,0:T(8,128)}, u32[]{:S(2)}) copy-start(f32[5,8,8192]{2,1,0:T(8,128)} %param.36) | copy-start | bytes 3932164
  4.2 11.0 %copy-start.19 = (s32[8,8192]{1,0:T(8,128)S(1)}, s32[8,8192]{1,0:T(8,128)}, u32[]{:S(2)}) copy-start(s32[8,8192]{1,0:T(8,128)} %param.42) | copy-start | bytes 786436
  5.4 25.0 %all-to-all-start = ((f32[5,64,128]{2,0,1:T(8,128)}), f32[5,64,128]{2,0,1:T(8,128)}, u32[]{:S(2)}, u32[]{:S(2)}) async-start(f32[5,64,128]{2,0,1:T(8,128)} %copy.64), calls=%async_computation | async-start | bytes 524288 | tf_op jit(solution)/shard_map/all_to_all | solution.py:159
  11.9 26.4 %collective-permute-start.4 = (f32[5,8,1]{2,1,0:T(8,128)S(1)}, f32[5,8,1]{2,1,0:T(8,128)S(1)}, u32[]{:S(2)}, u32[]{:S(2)}) collective-permute-start(f32[5,8,1]{2,1,0:T(8,128)S(1)} %get-tuple-element.1570), channel_id=1, source_target_pairs={{0,1},{1,2},{2,3},{3,0},{4,5},{5,6},{6,7},{7,4},{8,9},{9,10},{10,1... | collective-permute-start | bytes 488 | tf_op jit(solution)/shard_map/ppermute | solution.py:17
  13.1 25.3 %collective-permute-start.5 = (f32[5,8,1]{2,1,0:T(8,128)S(1)}, f32[5,8,1]{2,1,0:T(8,128)S(1)}, u32[]{:S(2)}, u32[]{:S(2)}) collective-permute-start(f32[5,8,1]{2,1,0:T(8,128)S(1)} %get-tuple-element.1571), channel_id=1, source_target_pairs={{1,0},{2,1},{3,2},{0,3},{5,4},{6,5},{7,6},{4,7},{9,8},{10,9},{11,1... | collective-permute-start | bytes 488 | tf_op jit(solution)/shard_map/ppermute | solution.py:19
  15.9 11.0 %copy-start.16 = (f32[5,8,8192]{2,1,0:T(8,128)S(1)}, f32[5,8,8192]{2,1,0:T(8,128)}, u32[]{:S(2)}) copy-start(f32[5,8,8192]{2,1,0:T(8,128)} %param.39) | copy-start | bytes 3932164
  26.9 1.3 copy-start.17
  28.2 2.1 copy-start.22
  80.2 2.6 copy-start.4
  82.8 8.1 %copy-start.5 = (f32[5,8192]{1,0:T(8,128)S(1)}, f32[5,8192]{1,0:T(8,128)}, u32[]{:S(2)}) copy-start(f32[5,8192]{1,0:T(8,128)} %get-tuple-element.2061) | copy-start | bytes 491524 | tf_op jit(solution)/shard_map/while
  82.8 7.6 collective-permute-start
  90.5 1.2 copy-start
  91.6 9.4 %copy-start.5 = (f32[5,8192]{1,0:T(8,128)S(1)}, f32[5,8192]{1,0:T(8,128)}, u32[]{:S(2)}) copy-start(f32[5,8192]{1,0:T(8,128)} %get-tuple-element.2061) | copy-start | bytes 491524 | tf_op jit(solution)/shard_map/while
  91.6 8.9 %collective-permute-start = (f32[5,8192]{1,0:T(8,128)}, f32[5,8192]{1,0:T(8,128)S(1)}, u32[]{:S(2)}, u32[]{:S(2)}) collective-permute-start(f32[5,8192]{1,0:T(8,128)} %get-tuple-element.2052), channel_id=1, source_target_pairs={{0,4},{4,8},{8,12},{12,16},{16,20},{20,24},{24,28},{1,5},{5,9},{9,... | collective-permute-start | bytes 491528 | tf_op jit(solution)/shard_map/while/body/eval_jaxpr/ppermute | solution.py:29
  100.6 1.2 copy-start
  101.7 9.4 %copy-start.5 = (f32[5,8192]{1,0:T(8,128)S(1)}, f32[5,8192]{1,0:T(8,128)}, u32[]{:S(2)}) copy-start(f32[5,8192]{1,0:T(8,128)} %get-tuple-element.2061) | copy-start | bytes 491524 | tf_op jit(solution)/shard_map/while
  101.7 8.9 %collective-permute-start = (f32[5,8192]{1,0:T(8,128)}, f32[5,8192]{1,0:T(8,128)S(1)}, u32[]{:S(2)}, u32[]{:S(2)}) collective-permute-start(f32[5,8192]{1,0:T(8,128)} %get-tuple-element.2052), channel_id=1, source_target_pairs={{0,4},{4,8},{8,12},{12,16},{16,20},{20,24},{24,28},{1,5},{5,9},{9,... | collective-permute-start | bytes 491528 | tf_op jit(solution)/shard_map/while/body/eval_jaxpr/ppermute | solution.py:29
  110.7 1.2 copy-start
  111.8 9.4 %copy-start.5 = (f32[5,8192]{1,0:T(8,128)S(1)}, f32[5,8192]{1,0:T(8,128)}, u32[]{:S(2)}) copy-start(f32[5,8192]{1,0:T(8,128)} %get-tuple-element.2061) | copy-start | bytes 491524 | tf_op jit(solution)/shard_map/while
  111.8 8.9 %collective-permute-start = (f32[5,8192]{1,0:T(8,128)}, f32[5,8192]{1,0:T(8,128)S(1)}, u32[]{:S(2)}, u32[]{:S(2)}) collective-permute-start(f32[5,8192]{1,0:T(8,128)} %get-tuple-element.2052), channel_id=1, source_target_pairs={{0,4},{4,8},{8,12},{12,16},{16,20},{20,24},{24,28},{1,5},{5,9},{9,... | collective-permute-start | bytes 491528 | tf_op jit(solution)/shard_map/while/body/eval_jaxpr/ppermute | solution.py:29
  120.8 1.2 copy-start
  121.9 9.4 %copy-start.5 = (f32[5,8192]{1,0:T(8,128)S(1)}, f32[5,8192]{1,0:T(8,128)}, u32[]{:S(2)}) copy-start(f32[5,8192]{1,0:T(8,128)} %get-tuple-element.2061) | copy-start | bytes 491524 | tf_op jit(solution)/shard_map/while
  121.9 8.9 %collective-permute-start = (f32[5,8192]{1,0:T(8,128)}, f32[5,8192]{1,0:T(8,128)S(1)}, u32[]{:S(2)}, u32[]{:S(2)}) collective-permute-start(f32[5,8192]{1,0:T(8,128)} %get-tuple-element.2052), channel_id=1, source_target_pairs={{0,4},{4,8},{8,12},{12,16},{16,20},{20,24},{24,28},{1,5},{5,9},{9,... | collective-permute-start | bytes 491528 | tf_op jit(solution)/shard_map/while/body/eval_jaxpr/ppermute | solution.py:29
  130.9 1.2 copy-start
  132.0 9.4 %copy-start.5 = (f32[5,8192]{1,0:T(8,128)S(1)}, f32[5,8192]{1,0:T(8,128)}, u32[]{:S(2)}) copy-start(f32[5,8192]{1,0:T(8,128)} %get-tuple-element.2061) | copy-start | bytes 491524 | tf_op jit(solution)/shard_map/while
  132.0 8.9 %collective-permute-start = (f32[5,8192]{1,0:T(8,128)}, f32[5,8192]{1,0:T(8,128)S(1)}, u32[]{:S(2)}, u32[]{:S(2)}) collective-permute-start(f32[5,8192]{1,0:T(8,128)} %get-tuple-element.2052), channel_id=1, source_target_pairs={{0,4},{4,8},{8,12},{12,16},{16,20},{20,24},{24,28},{1,5},{5,9},{9,... | collective-permute-start | bytes 491528 | tf_op jit(solution)/shard_map/while/body/eval_jaxpr/ppermute | solution.py:29
  142.1 9.4 %copy-start.5 = (f32[5,8192]{1,0:T(8,128)S(1)}, f32[5,8192]{1,0:T(8,128)}, u32[]{:S(2)}) copy-start(f32[5,8192]{1,0:T(8,128)} %get-tuple-element.2061) | copy-start | bytes 491524 | tf_op jit(solution)/shard_map/while
  142.1 8.9 %collective-permute-start = (f32[5,8192]{1,0:T(8,128)}, f32[5,8192]{1,0:T(8,128)S(1)}, u32[]{:S(2)}, u32[]{:S(2)}) collective-permute-start(f32[5,8192]{1,0:T(8,128)} %get-tuple-element.2052), channel_id=1, source_target_pairs={{0,4},{4,8},{8,12},{12,16},{16,20},{20,24},{24,28},{1,5},{5,9},{9,... | collective-permute-start | bytes 491528 | tf_op jit(solution)/shard_map/while/body/eval_jaxpr/ppermute | solution.py:29
  152.2 9.4 %copy-start.5 = (f32[5,8192]{1,0:T(8,128)S(1)}, f32[5,8192]{1,0:T(8,128)}, u32[]{:S(2)}) copy-start(f32[5,8192]{1,0:T(8,128)} %get-tuple-element.2061) | copy-start | bytes 491524 | tf_op jit(solution)/shard_map/while
  152.2 8.9 %collective-permute-start = (f32[5,8192]{1,0:T(8,128)}, f32[5,8192]{1,0:T(8,128)S(1)}, u32[]{:S(2)}, u32[]{:S(2)}) collective-permute-start(f32[5,8192]{1,0:T(8,128)} %get-tuple-element.2052), channel_id=1, source_target_pairs={{0,4},{4,8},{8,12},{12,16},{16,20},{20,24},{24,28},{1,5},{5,9},{9,... | collective-permute-start | bytes 491528 | tf_op jit(solution)/shard_map/while/body/eval_jaxpr/ppermute | solution.py:29
  251.5 9.4 %collective-permute-start.1 = (f32[5,8192]{1,0:T(8,128)}, f32[5,8192]{1,0:T(8,128)S(1)}, u32[]{:S(2)}, u32[]{:S(2)}) collective-permute-start(f32[5,8192]{1,0:T(8,128)} %get-tuple-element.2124), channel_id=1, source_target_pairs={{4,0},{8,4},{12,8},{16,12},{20,16},{24,20},{28,24},{5,1},{9,5},{13... | collective-permute-start | bytes 491528 | tf_op jit(solution)/shard_map/while/body/eval_jaxpr/ppermute | solution.py:29
  262.1 8.8 %collective-permute-start.1 = (f32[5,8192]{1,0:T(8,128)}, f32[5,8192]{1,0:T(8,128)S(1)}, u32[]{:S(2)}, u32[]{:S(2)}) collective-permute-start(f32[5,8192]{1,0:T(8,128)} %get-tuple-element.2124), channel_id=1, source_target_pairs={{4,0},{8,4},{12,8},{16,12},{20,16},{24,20},{28,24},{5,1},{9,5},{13... | collective-permute-start | bytes 491528 | tf_op jit(solution)/shard_map/while/body/eval_jaxpr/ppermute | solution.py:29
  272.1 8.8 %collective-permute-start.1 = (f32[5,8192]{1,0:T(8,128)}, f32[5,8192]{1,0:T(8,128)S(1)}, u32[]{:S(2)}, u32[]{:S(2)}) collective-permute-start(f32[5,8192]{1,0:T(8,128)} %get-tuple-element.2124), channel_id=1, source_target_pairs={{4,0},{8,4},{12,8},{16,12},{20,16},{24,20},{28,24},{5,1},{9,5},{13... | collective-permute-start | bytes 491528 | tf_op jit(solution)/shard_map/while/body/eval_jaxpr/ppermute | solution.py:29
  282.1 8.8 %collective-permute-start.1 = (f32[5,8192]{1,0:T(8,128)}, f32[5,8192]{1,0:T(8,128)S(1)}, u32[]{:S(2)}, u32[]{:S(2)}) collective-permute-start(f32[5,8192]{1,0:T(8,128)} %get-tuple-element.2124), channel_id=1, source_target_pairs={{4,0},{8,4},{12,8},{16,12},{20,16},{24,20},{28,24},{5,1},{9,5},{13... | collective-permute-start | bytes 491528 | tf_op jit(solution)/shard_map/while/body/eval_jaxpr/ppermute | solution.py:29
  292.0 8.8 %collective-permute-start.1 = (f32[5,8192]{1,0:T(8,128)}, f32[5,8192]{1,0:T(8,128)S(1)}, u32[]{:S(2)}, u32[]{:S(2)}) collective-permute-start(f32[5,8192]{1,0:T(8,128)} %get-tuple-element.2124), channel_id=1, source_target_pairs={{4,0},{8,4},{12,8},{16,12},{20,16},{24,20},{28,24},{5,1},{9,5},{13... | collective-permute-start | bytes 491528 | tf_op jit(solution)/shard_map/while/body/eval_jaxpr/ppermute | solution.py:29
  302.0 8.8 %collective-permute-start.1 = (f32[5,8192]{1,0:T(8,128)}, f32[5,8192]{1,0:T(8,128)S(1)}, u32[]{:S(2)}, u32[]{:S(2)}) collective-permute-start(f32[5,8192]{1,0:T(8,128)} %get-tuple-element.2124), channel_id=1, source_target_pairs={{4,0},{8,4},{12,8},{16,12},{20,16},{24,20},{28,24},{5,1},{9,5},{13... | collective-permute-start | bytes 491528 | tf_op jit(solution)/shard_map/while/body/eval_jaxpr/ppermute | solution.py:29
  311.9 8.8 %collective-permute-start.1 = (f32[5,8192]{1,0:T(8,128)}, f32[5,8192]{1,0:T(8,128)S(1)}, u32[]{:S(2)}, u32[]{:S(2)}) collective-permute-start(f32[5,8192]{1,0:T(8,128)} %get-tuple-element.2124), channel_id=1, source_target_pairs={{4,0},{8,4},{12,8},{16,12},{20,16},{24,20},{28,24},{5,1},{9,5},{13... | collective-permute-start | bytes 491528 | tf_op jit(solution)/shard_map/while/body/eval_jaxpr/ppermute | solution.py:29
  321.9 8.8 %collective-permute-start.1 = (f32[5,8192]{1,0:T(8,128)}, f32[5,8192]{1,0:T(8,128)S(1)}, u32[]{:S(2)}, u32[]{:S(2)}) collective-permute-start(f32[5,8192]{1,0:T(8,128)} %get-tuple-element.2124), channel_id=1, source_target_pairs={{4,0},{8,4},{12,8},{16,12},{20,16},{24,20},{28,24},{5,1},{9,5},{13... | collective-permute-start | bytes 491528 | tf_op jit(solution)/shard_map/while/body/eval_jaxpr/ppermute | solution.py:29
  333.0 82.2 %copy-start.12 = (f32[5,8,8192]{2,1,0:T(8,128)S(1)}, f32[5,8,8192]{2,1,0:T(8,128)}, u32[]{:S(2)}) copy-start(f32[5,8,8192]{2,1,0:T(8,128)} %param.36) | copy-start | bytes 3932164
  419.8 13.1 %all-to-all-start.1 = ((f32[5,64,128]{2,0,1:T(8,128)}), f32[5,64,128]{2,0,1:T(8,128)S(1)}, u32[]{:S(2)}, u32[]{:S(2)}) async-start(f32[5,64,128]{2,0,1:T(8,128)} %copy.77), calls=%async_computation.1 | async-start | bytes 524288 | tf_op jit(solution)/shard_map/all_to_all | solution.py:159
  422.7 13.9 %collective-permute-start.6 = (f32[5,8,1]{2,1,0:T(8,128)S(1)}, f32[5,8,1]{2,1,0:T(8,128)S(1)}, u32[]{:S(2)}, u32[]{:S(2)}) collective-permute-start(f32[5,8,1]{2,1,0:T(8,128)S(1)} %get-tuple-element.1568), channel_id=1, source_target_pairs={{0,1},{1,2},{2,3},{3,0},{4,5},{5,6},{6,7},{7,4},{8,9},{9,10},{10,1... | collective-permute-start | bytes 488 | tf_op jit(solution)/shard_map/ppermute | solution.py:17
  423.9 12.8 %collective-permute-start.7 = (f32[5,8,1]{2,1,0:T(8,128)S(1)}, f32[5,8,1]{2,1,0:T(8,128)S(1)}, u32[]{:S(2)}, u32[]{:S(2)}) collective-permute-start(f32[5,8,1]{2,1,0:T(8,128)S(1)} %get-tuple-element.1569), channel_id=1, source_target_pairs={{1,0},{2,1},{3,2},{0,3},{5,4},{6,5},{7,6},{4,7},{9,8},{10,9},{11,1... | collective-permute-start | bytes 488 | tf_op jit(solution)/shard_map/ppermute | solution.py:19
  435.1 1.6 copy-start.15
  435.1 1.6 copy-start.18
  480.6 6.6 collective-permute-start.2
  488.3 8.8 %collective-permute-start.2 = (f32[5,8192]{1,0:T(8,128)}, f32[5,8192]{1,0:T(8,128)S(1)}, u32[]{:S(2)}, u32[]{:S(2)}) collective-permute-start(f32[5,8192]{1,0:T(8,128)} %get-tuple-element.2193), channel_id=1, source_target_pairs={{0,4},{4,8},{8,12},{12,16},{16,20},{20,24},{24,28},{1,5},{5,9},{9,... | collective-permute-start | bytes 491528 | tf_op jit(solution)/shard_map/while/body/eval_jaxpr/ppermute | solution.py:29
  498.3 8.8 %collective-permute-start.2 = (f32[5,8192]{1,0:T(8,128)}, f32[5,8192]{1,0:T(8,128)S(1)}, u32[]{:S(2)}, u32[]{:S(2)}) collective-permute-start(f32[5,8192]{1,0:T(8,128)} %get-tuple-element.2193), channel_id=1, source_target_pairs={{0,4},{4,8},{8,12},{12,16},{16,20},{20,24},{24,28},{1,5},{5,9},{9,... | collective-permute-start | bytes 491528 | tf_op jit(solution)/shard_map/while/body/eval_jaxpr/ppermute | solution.py:29
  508.2 8.8 %collective-permute-start.2 = (f32[5,8192]{1,0:T(8,128)}, f32[5,8192]{1,0:T(8,128)S(1)}, u32[]{:S(2)}, u32[]{:S(2)}) collective-permute-start(f32[5,8192]{1,0:T(8,128)} %get-tuple-element.2193), channel_id=1, source_target_pairs={{0,4},{4,8},{8,12},{12,16},{16,20},{20,24},{24,28},{1,5},{5,9},{9,... | collective-permute-start | bytes 491528 | tf_op jit(solution)/shard_map/while/body/eval_jaxpr/ppermute | solution.py:29
  518.2 8.8 %collective-permute-start.2 = (f32[5,8192]{1,0:T(8,128)}, f32[5,8192]{1,0:T(8,128)S(1)}, u32[]{:S(2)}, u32[]{:S(2)}) collective-permute-start(f32[5,8192]{1,0:T(8,128)} %get-tuple-element.2193), channel_id=1, source_target_pairs={{0,4},{4,8},{8,12},{12,16},{16,20},{20,24},{24,28},{1,5},{5,9},{9,... | collective-permute-start | bytes 491528 | tf_op jit(solution)/shard_map/while/body/eval_jaxpr/ppermute | solution.py:29
  528.1 8.8 %collective-permute-start.2 = (f32[5,8192]{1,0:T(8,128)}, f32[5,8192]{1,0:T(8,128)S(1)}, u32[]{:S(2)}, u32[]{:S(2)}) collective-permute-start(f32[5,8192]{1,0:T(8,128)} %get-tuple-element.2193), channel_id=1, source_target_pairs={{0,4},{4,8},{8,12},{12,16},{16,20},{20,24},{24,28},{1,5},{5,9},{9,... | collective-permute-start | bytes 491528 | tf_op jit(solution)/shard_map/while/body/eval_jaxpr/ppermute | solution.py:29
  538.1 8.8 %collective-permute-start.2 = (f32[5,8192]{1,0:T(8,128)}, f32[5,8192]{1,0:T(8,128)S(1)}, u32[]{:S(2)}, u32[]{:S(2)}) collective-permute-start(f32[5,8192]{1,0:T(8,128)} %get-tuple-element.2193), channel_id=1, source_target_pairs={{0,4},{4,8},{8,12},{12,16},{16,20},{20,24},{24,28},{1,5},{5,9},{9,... | collective-permute-start | bytes 491528 | tf_op jit(solution)/shard_map/while/body/eval_jaxpr/ppermute | solution.py:29
  548.1 8.8 %collective-permute-start.2 = (f32[5,8192]{1,0:T(8,128)}, f32[5,8192]{1,0:T(8,128)S(1)}, u32[]{:S(2)}, u32[]{:S(2)}) collective-permute-start(f32[5,8192]{1,0:T(8,128)} %get-tuple-element.2193), channel_id=1, source_target_pairs={{0,4},{4,8},{8,12},{12,16},{16,20},{20,24},{24,28},{1,5},{5,9},{9,... | collective-permute-start | bytes 491528 | tf_op jit(solution)/shard_map/while/body/eval_jaxpr/ppermute | solution.py:29
  657.8 9.4 %collective-permute-start.3 = (f32[5,8192]{1,0:T(8,128)}, f32[5,8192]{1,0:T(8,128)S(1)}, u32[]{:S(2)}, u32[]{:S(2)}) collective-permute-start(f32[5,8192]{1,0:T(8,128)} %get-tuple-element.2265), channel_id=1, source_target_pairs={{4,0},{8,4},{12,8},{16,12},{20,16},{24,20},{28,24},{5,1},{9,5},{13... | collective-permute-start | bytes 491528 | tf_op jit(solution)/shard_map/while/body/eval_jaxpr/ppermute | solution.py:29
  668.4 8.8 %collective-permute-start.3 = (f32[5,8192]{1,0:T(8,128)}, f32[5,8192]{1,0:T(8,128)S(1)}, u32[]{:S(2)}, u32[]{:S(2)}) collective-permute-start(f32[5,8192]{1,0:T(8,128)} %get-tuple-element.2265), channel_id=1, source_target_pairs={{4,0},{8,4},{12,8},{16,12},{20,16},{24,20},{28,24},{5,1},{9,5},{13... | collective-permute-start | bytes 491528 | tf_op jit(solution)/shard_map/while/body/eval_jaxpr/ppermute | solution.py:29
  678.3 8.8 %collective-permute-start.3 = (f32[5,8192]{1,0:T(8,128)}, f32[5,8192]{1,0:T(8,128)S(1)}, u32[]{:S(2)}, u32[]{:S(2)}) collective-permute-start(f32[5,8192]{1,0:T(8,128)} %get-tuple-element.2265), channel_id=1, source_target_pairs={{4,0},{8,4},{12,8},{16,12},{20,16},{24,20},{28,24},{5,1},{9,5},{13... | collective-permute-start | bytes 491528 | tf_op jit(solution)/shard_map/while/body/eval_jaxpr/ppermute | solution.py:29
  688.3 8.8 %collective-permute-start.3 = (f32[5,8192]{1,0:T(8,128)}, f32[5,8192]{1,0:T(8,128)S(1)}, u32[]{:S(2)}, u32[]{:S(2)}) collective-permute-start(f32[5,8192]{1,0:T(8,128)} %get-tuple-element.2265), channel_id=1, source_target_pairs={{4,0},{8,4},{12,8},{16,12},{20,16},{24,20},{28,24},{5,1},{9,5},{13... | collective-permute-start | bytes 491528 | tf_op jit(solution)/shard_map/while/body/eval_jaxpr/ppermute | solution.py:29
  698.3 8.8 %collective-permute-start.3 = (f32[5,8192]{1,0:T(8,128)}, f32[5,8192]{1,0:T(8,128)S(1)}, u32[]{:S(2)}, u32[]{:S(2)}) collective-permute-start(f32[5,8192]{1,0:T(8,128)} %get-tuple-element.2265), channel_id=1, source_target_pairs={{4,0},{8,4},{12,8},{16,12},{20,16},{24,20},{28,24},{5,1},{9,5},{13... | collective-permute-start | bytes 491528 | tf_op jit(solution)/shard_map/while/body/eval_jaxpr/ppermute | solution.py:29
  708.2 8.8 %collective-permute-start.3 = (f32[5,8192]{1,0:T(8,128)}, f32[5,8192]{1,0:T(8,128)S(1)}, u32[]{:S(2)}, u32[]{:S(2)}) collective-permute-start(f32[5,8192]{1,0:T(8,128)} %get-tuple-element.2265), channel_id=1, source_target_pairs={{4,0},{8,4},{12,8},{16,12},{20,16},{24,20},{28,24},{5,1},{9,5},{13... | collective-permute-start | bytes 491528 | tf_op jit(solution)/shard_map/while/body/eval_jaxpr/ppermute | solution.py:29
  718.2 8.8 %collective-permute-start.3 = (f32[5,8192]{1,0:T(8,128)}, f32[5,8192]{1,0:T(8,128)S(1)}, u32[]{:S(2)}, u32[]{:S(2)}) collective-permute-start(f32[5,8192]{1,0:T(8,128)} %get-tuple-element.2265), channel_id=1, source_target_pairs={{4,0},{8,4},{12,8},{16,12},{20,16},{24,20},{28,24},{5,1},{9,5},{13... | collective-permute-start | bytes 491528 | tf_op jit(solution)/shard_map/while/body/eval_jaxpr/ppermute | solution.py:29
  728.1 8.8 %collective-permute-start.3 = (f32[5,8192]{1,0:T(8,128)}, f32[5,8192]{1,0:T(8,128)S(1)}, u32[]{:S(2)}, u32[]{:S(2)}) collective-permute-start(f32[5,8192]{1,0:T(8,128)} %get-tuple-element.2265), channel_id=1, source_target_pairs={{4,0},{8,4},{12,8},{16,12},{20,16},{24,20},{28,24},{5,1},{9,5},{13... | collective-permute-start | bytes 491528 | tf_op jit(solution)/shard_map/while/body/eval_jaxpr/ppermute | solution.py:29
  804.9 1.5 copy-start.14
  (34 other events, 38.4 us)
where the time goes:
time: 813 us; the launch traced here: 806 us
  other arithmetic  254 us (31%)
  local copies, waits for them, and re-layouts  238 us (29%)
  waiting for transfers between devices  176 us (22%)
  starting transfers between devices  127 us (16%)
    ppermute x32, waiting for transfers between devices, passed_along(): lax.ppermute(value, axis, [(source, source + steps) for source in range(i...  169 us
    dynamic_slice x48, local copies, waits for them, and re-layouts, plane_of(): return lax.dynamic_index_in_dim(array, index, axis, keepdims=False)  129 us
    reduce_sum x96, other arithmetic, apply_block(): return jnp.sum(block_inv * vector[None], axis=1)  116 us
    ppermute x32, starting transfers between devices, passed_along(): lax.ppermute(value, axis, [(source, source + steps) for source in range(i...  111 us
    dynamic_update_slice x32, local copies, waits for them, and re-layouts, step(): return (face, lax.dynamic_update_index_in_dim(sweep_output, face, index, 1))  54.3 us
    unnamed x46, local copies, waits for them, and re-layouts  22.3 us
    reduce_sum x32, other arithmetic, multiply_maps(): return jnp.sum(left[:, :, None, :] * right[None], axis=1)  21.3 us
    add x16, other arithmetic, step(): plane_of(driving_term, index, 1) + plane_of(decay, index, 1) * face  17.3 us
  transfers between devices with their start and end apart: 38, of which 33 were waited for; matrix products, arithmetic and copies ran while one was open for 3% of the time, Pallas kernels for 0%

commit v1 on v0

v1 whole, which is shorter than its diff:
```python
import functools

import jax
import jax.numpy as jnp
from jax import lax
from jax.experimental import pallas as pl
from jax.experimental.pallas import tpu as pltpu
from jax.sharding import PartitionSpec as P

ITERS = 2
CAP = 2
NV = 5
SLOT_ROWS = 16
STEP = 16
CHUNKS = 4
MESH = pl.DeviceIdType.MESH
PAIRS = [(a, b) for a in range(NV) for b in range(a, NV)]


def pair(a, b):
    return PAIRS.index((min(a, b), max(a, b)))


def split3(x):
    high = x.astype(jnp.bfloat16)
    rest = x - high.astype(jnp.float32)
    mid = rest.astype(jnp.bfloat16)
    low = (rest - mid.astype(jnp.float32)).astype(jnp.bfloat16)
    return jnp.concatenate([high, mid, low], axis=0)


def iota(shape, dim):
    return lax.broadcasted_iota(jnp.int32, shape, dim)


def kernel(
    ns, nc, planes, tiles,
    state_h, forcing_h, inverse_h, lower_h, upper_h, coupling_h, blank_h,
    receiver_r, block_s, offset_r, weight_r, target_r,
    final_h, update_h,
    state, forcing, inverse, lower, upper, coupling, blank,
    near, update, gathered, placed, outgoing, received, pick, stacked,
    edge_out, edge_in, face,
    load_sem, out_sem, own_sem, fsend, frecv, esend, erecv, wsend, wrecv,
):
    s, c = lax.axis_index("stream"), lax.axis_index("cross")
    devices = ns * nc
    me = s * nc + c
    senders = block_s.shape[0]
    slots = devices * CAP
    span = tiles // CHUNKS

    loads = []

    def load(source, target):
        copy = pltpu.make_async_copy(source, target, load_sem.at[len(loads)])
        copy.start()
        loads.append(copy)
        return copy

    def rows_of(i):
        return pl.ds(i * tiles, tiles)

    state_loads = [load(state_h.at[:, :, i, :], state.at[:, rows_of(i), :]) for i in range(planes)]
    drive_loads = []
    for i in range(planes):
        drive_loads.append(load(forcing_h.at[:, :, i, :], forcing.at[:, rows_of(i), :]))
        drive_loads.append(load(coupling_h.at[:, i, :], coupling.at[rows_of(i), :]))
        drive_loads.append(load(blank_h.at[:, i, :], blank.at[rows_of(i), :]))
    sweep_loads = []
    for i in range(planes):
        sweep_loads.append(load(lower_h.at[:, :, i, :], lower.at[:, rows_of(i), :]))
        for a in range(NV):
            first = pair(a, a)
            sweep_loads.append(
                load(
                    inverse_h.at[a, pl.ds(a, NV - a), :, i, :],
                    inverse.at[pl.ds(first, NV - a), rows_of(i), :],
                )
            )
    for i in range(planes):
        sweep_loads.append(load(upper_h.at[:, :, i, :], upper.at[:, rows_of(i), :]))

    barrier = pltpu.get_barrier_semaphore()

    def greet(k, carry):
        other = lax.rem(me + k, devices)
        pl.semaphore_signal(
            barrier, inc=1, device_id=(other // nc, lax.rem(other, nc)), device_id_type=MESH
        )
        return carry

    lax.fori_loop(1, devices, greet, 0)

    eye = iota((senders, senders), 0) == iota((senders, senders), 1)
    recv_col = receiver_r[...].astype(jnp.float32)
    recv_row = jnp.sum(jnp.where(eye, recv_col, 0.0), axis=0, keepdims=True)
    earlier = iota((senders, senders), 0) < iota((senders, senders), 1)
    rank_row = jnp.sum(
        jnp.where(earlier & (recv_col == recv_row), 1.0, 0.0), axis=0, keepdims=True
    )
    key_row = rank_row * devices + recv_row
    place = (key_row == iota((slots, senders), 0).astype(jnp.float32)).astype(jnp.float32)
    place3 = jnp.concatenate([place, place, place], axis=1).astype(jnp.bfloat16)
    offset_col = jnp.sum(
        jnp.where(eye, offset_r[...].astype(jnp.float32), 0.0), axis=1, keepdims=True
    ).astype(jnp.int32)
    offset_all = jnp.broadcast_to(offset_col, (senders, 128))

    slot_eye = iota((slots, slots), 0) == iota((slots, slots), 1)
    target_col = jnp.sum(
        jnp.where(slot_eye, target_r[...].astype(jnp.float32), 0.0), axis=1, keepdims=True
    )
    slot_k = iota((slots, slots), 1)
    wanted = jnp.where(slot_k < devices, slot_k * CAP, (slot_k - devices) * CAP + 1)
    target_row = jnp.sum(
        jnp.where(iota((slots, slots), 0) == wanted, target_col, 0.0), axis=0, keepdims=True
    )
    target3 = jnp.concatenate([target_row, target_row, target_row], axis=1)

    def fill(i, carry):
        ids = (iota((tiles, 3 * slots), 0) + i * tiles).astype(jnp.float32)
        pick[pl.ds(pl.multiple_of(i * tiles, tiles), tiles), :] = jnp.where(
            ids == target3, 1.0, 0.0
        ).astype(jnp.bfloat16)
        return carry

    lax.fori_loop(0, planes, fill, 0)
    for it in range(ITERS):
        for r in range(NV * CAP, SLOT_ROWS):
            outgoing[it, pl.ds(r, devices, stride=SLOT_ROWS), :] = jnp.zeros(
                (devices, 128), jnp.float32
            )

    for copy in state_loads:
        copy.wait()
    pl.semaphore_wait(barrier, devices - 1)

    def fringe_copy(it, k):
        other = lax.rem(me + k, devices)
        start = pl.multiple_of(other * SLOT_ROWS, SLOT_ROWS)
        mine = pl.multiple_of(me * SLOT_ROWS, SLOT_ROWS)
        return pltpu.make_async_remote_copy(
            src_ref=outgoing.at[it, pl.ds(start, SLOT_ROWS), :],
            dst_ref=received.at[it, pl.ds(mine, SLOT_ROWS), :],
            send_sem=fsend.at[it, k],
            recv_sem=frecv.at[it, k],
            device_id=(other // nc, lax.rem(other, nc)),
            device_id_type=MESH,
        )

    def edge_copy(it, side):
        other = lax.rem(c + 1, nc) if side == 0 else lax.rem(c + nc - 1, nc)
        return pltpu.make_async_remote_copy(
            src_ref=edge_out.at[it, side],
            dst_ref=edge_in.at[it, side],
            send_sem=esend.at[it, side],
            recv_sem=erecv.at[it, side],
            device_id=(s, other),
            device_id_type=MESH,
        )

    def wave_copy(it, down, part):
        rows = pl.ds(part * span, span)
        if down:
            source = near.at[:, pl.ds((planes - 1) * tiles + part * span, span), :]
            other = lax.rem(s + 1, ns)
        else:
            source = update.at[:, rows, :]
            other = lax.rem(s + ns - 1, ns)
        way = 0 if down else 1
        return pltpu.make_async_remote_copy(
            src_ref=source,
            dst_ref=face.at[it, way, :, rows, :],
            send_sem=wsend.at[it, way, part],
            recv_sem=wrecv.at[it, way, part],
            device_id=(other, c),
            device_id_type=MESH,
        )

    def start_face(it, way, part):
        at_end = (s == 0) if way == 0 else (s == ns - 1)

        @pl.when(at_end)
        def _():
            face[it, way, :, pl.ds(part * span, span), :] = jnp.zeros(
                (NV, span, 128), jnp.float32
            )

        @pl.when(jnp.logical_not(at_end))
        def _():
            wave_copy(it, way == 0, part).wait_recv()

    def apply(rows, vector):
        out = []
        for a in range(NV):
            total = None
            for b in range(NV):
                term = inverse[pair(a, b), rows, :] * vector[b]
                total = term if total is None else total + term
            out.append(total)
        return out

    def sweep_down(it, part):
        start_face(it, 0, part)

        def step(g, carry):
            base = part * span + g * STEP
            x = [face[it, 0, v, pl.ds(base, STEP), :] for v in range(NV)]
            for i in range(planes):
                rows = pl.ds(i * tiles + base, STEP)
                t = [near[v, rows, :] + lower[v, rows, :] * x[v] for v in range(NV)]
                x = apply(rows, t)
                for v in range(NV):
                    near[v, rows, :] = x[v]
            return carry

        for g in range(span // STEP):
            step(g, 0)

        @pl.when(s < ns - 1)
        def _():
            wave_copy(it, True, part).start()

    def out_copies(part):
        copies = []
        for i in range(planes):
            rows = pl.ds(i * tiles + part * span, span)
            for n, (source, target) in enumerate(((state, final_h), (update, update_h))):
                copies.append(
                    pltpu.make_async_copy(
                        source.at[:, rows, :],
                        target.at[:, pl.ds(part * span, span), i, :],
                        out_sem.at[part, i, n],
                    )
                )
        return copies

    def sweep_up(it, part):
        start_face(it, 1, part)

        def step(g, carry):
            base = part * span + g * STEP
            y = [face[it, 1, v, pl.ds(base, STEP), :] for v in range(NV)]
            for i in reversed(range(planes)):
                rows = pl.ds(i * tiles + base, STEP)
                t = [upper[v, rows, :] * y[v] for v in range(NV)]
                z = apply(rows, t)
                y = [near[v, rows, :] + z[v] for v in range(NV)]
                for v in range(NV):
                    update[v, rows, :] = y[v]
                    state[v, rows, :] = state[v, rows, :] + y[v]
            return carry

        for g in range(span // STEP):
            step(g, 0)

        @pl.when(s > 0)
        def _():
            wave_copy(it, False, part).start()

        if it == ITERS - 1:
            for copy in out_copies(part):
                copy.start()

    for it in range(ITERS):
        for v in range(NV):
            edge_out[it, 0, v] = state[v, pl.ds(tiles - 1, planes, stride=tiles), :]
            edge_out[it, 1, v] = state[v, pl.ds(0, planes, stride=tiles), :]
        for side in range(2):
            edge_copy(it, side).start()

        def gather(q, carry):
            for k in range(8):
                e = q * 8 + k
                block = block_s[e]
                for v in range(NV):
                    gathered[v, pl.ds(e, 1), :] = state[v, pl.ds(block, 1), :]
            return carry

        lax.fori_loop(0, senders // 8, gather, 0)
        weight = weight_r[...]
        for v in range(NV):
            chosen = gathered[v]
            moved = chosen
            for bit in range(7):
                rolled = pltpu.roll(moved, 128 - (1 << bit), 1)
                moved = jnp.where((offset_all & (1 << bit)) != 0, rolled, moved)
            placed[:, v * 128:(v + 1) * 128] = split3(weight * (chosen + moved))
        slot_values = jnp.dot(place3, placed[...], preferred_element_type=jnp.float32)
        for v in range(NV):
            for k in range(CAP):
                outgoing[it, pl.ds(v * CAP + k, devices, stride=SLOT_ROWS), :] = slot_values[
                    k * devices:(k + 1) * devices, v * 128:(v + 1) * 128
                ]

        def send(k, carry):
            fringe_copy(it, k).start()
            return carry

        lax.fori_loop(1, devices, send, 0)
        mine = pl.ds(pl.multiple_of(me * SLOT_ROWS, SLOT_ROWS), SLOT_ROWS)
        received[it, mine, :] = outgoing[it, mine, :]

        if it == 0:
            for copy in drive_loads:
                copy.wait()
        else:
            for part in range(CHUNKS):
                @pl.when(s < ns - 1)
                def _():
                    wave_copy(it - 1, True, part).wait_send()

                @pl.when(s > 0)
                def _():
                    wave_copy(it - 1, False, part).wait_send()
        for side in range(2):
            edge_copy(it, side).wait_recv()
        lane = iota((tiles, 128), 1)
        row = iota((tiles, 128), 0)

        def drive(i, carry):
            rows = pl.ds(pl.multiple_of(i * tiles, tiles), tiles)
            factor = coupling[rows, :]
            for v in range(NV):
                x = state[v, rows, :]
                before = pltpu.roll(edge_in[it, 0, v, pl.ds(i, 1), :], 1, 1)
                after = pltpu.roll(edge_in[it, 1, v, pl.ds(i, 1), :], 127, 1)
                left = pltpu.roll(x, 1, 1)
                left = jnp.where(
                    lane == 0, jnp.where(row == 0, before, pltpu.roll(left, 1, 0)), left
                )
                right = pltpu.roll(x, 127, 1)
                right = jnp.where(
                    lane == 127,
                    jnp.where(row == tiles - 1, after, pltpu.roll(right, tiles - 1, 0)),
                    right,
                )
                near[v, rows, :] = forcing[v, rows, :] - factor * (2.0 * x - left - right)
            return carry

        lax.fori_loop(0, planes, drive, 0)

        def take(k, carry):
            fringe_copy(it, k).wait_recv()
            return carry

        lax.fori_loop(1, devices, take, 0)
        for v in range(NV):
            parts = [
                received[it, pl.ds(v * CAP + k, devices, stride=SLOT_ROWS), :] for k in range(CAP)
            ]
            stacked[:, v * 128:(v + 1) * 128] = split3(jnp.concatenate(parts, axis=0))

        def add_fringe(i, carry):
            rows = pl.ds(pl.multiple_of(i * tiles, tiles), tiles)
            hole = (1 - blank[rows, :]).astype(jnp.float32)
            fringe = jnp.dot(pick[rows, :], stacked[...], preferred_element_type=jnp.float32)
            for v in range(NV):
                near[v, rows, :] = near[v, rows, :] + hole * fringe[:, v * 128:(v + 1) * 128]
            return carry

        lax.fori_loop(0, planes, add_fringe, 0)

        if it == 0:
            for copy in sweep_loads:
                copy.wait()
        for part in range(CHUNKS):
            sweep_down(it, part)

            @pl.when(s == ns - 1)
            def _():
                sweep_up(it, part)

        @pl.when(s < ns - 1)
        def _():
            for part in range(CHUNKS):
                sweep_up(it, part)

        for side in range(2):
            edge_copy(it, side).wait_send()

        def sent(k, carry):
            fringe_copy(it, k).wait_send()
            return carry

        lax.fori_loop(1, devices, sent, 0)

    for part in range(CHUNKS):
        @pl.when(s < ns - 1)
        def _():
            wave_copy(ITERS - 1, True, part).wait_send()

        @pl.when(s > 0)
        def _():
            wave_copy(ITERS - 1, False, part).wait_send()

        for copy in out_copies(part):
            copy.wait()


def shards(
    initial_state, forcing, block_inverse, lower_decay, upper_decay, cross_coupling, iblank,
    donor_receiver, donor_block, stencil_offset, stencil_weight, fringe_target,
):
    ns, nc = lax.axis_size("stream"), lax.axis_size("cross")
    devices = ns * nc
    planes, cells = initial_state.shape[1:]
    tiles = cells // 128
    senders = donor_block.shape[0]
    slots = devices * CAP

    def tiled(x):
        lead = x.shape[:-2]
        n = len(lead)
        order = tuple(range(n)) + (n + 1, n, n + 2)
        return x.reshape(lead + (planes, tiles, 128)).transpose(order)

    def untiled(x):
        return x.transpose(0, 2, 1, 3).reshape(NV, planes, cells)

    full = (NV, planes * tiles, 128)
    f32, bf16 = jnp.float32, jnp.bfloat16
    dma = pltpu.SemaphoreType.DMA
    out = jax.ShapeDtypeStruct((NV, tiles, planes, 128), f32)
    hbm = pl.BlockSpec(memory_space=pl.ANY)
    vmem = pl.BlockSpec(memory_space=pltpu.VMEM)
    smem = pl.BlockSpec(memory_space=pltpu.SMEM)
    final, update = pl.pallas_call(
        functools.partial(kernel, ns, nc, planes, tiles),
        out_shape=(out, out),
        in_specs=[hbm] * 7 + [vmem, smem, vmem, vmem, vmem],
        out_specs=(hbm, hbm),
        scratch_shapes=[
            pltpu.VMEM(full, f32),
            pltpu.VMEM(full, f32),
            pltpu.VMEM((len(PAIRS),) + full[1:], f32),
            pltpu.VMEM(full, f32),
            pltpu.VMEM(full, f32),
            pltpu.VMEM(full[1:], f32),
            pltpu.VMEM(full[1:], jnp.int32),
            pltpu.VMEM(full, f32),
            pltpu.VMEM(full, f32),
            pltpu.VMEM((NV, senders, 128), f32),
            pltpu.VMEM((3 * senders, NV * 128), bf16),
            pltpu.VMEM((ITERS, devices * SLOT_ROWS, 128), f32),
            pltpu.VMEM((ITERS, devices * SLOT_ROWS, 128), f32),
            pltpu.VMEM((planes * tiles, 3 * slots), bf16),
            pltpu.VMEM((3 * slots, NV * 128), bf16),
            pltpu.VMEM((ITERS, 2, NV, planes, 128), f32),
            pltpu.VMEM((ITERS, 2, NV, planes, 128), f32),
            pltpu.VMEM((ITERS, 2, NV, tiles, 128), f32),
            dma((planes * (4 + 2 + NV),)),
            dma((CHUNKS, planes, 2)),
            dma((1,)),
            dma((ITERS, devices)),
            dma((ITERS, devices)),
            dma((ITERS, 2)),
            dma((ITERS, 2)),
            dma((ITERS, 2, CHUNKS)),
            dma((ITERS, 2, CHUNKS)),
        ],
        compiler_params=pltpu.CompilerParams(
            collective_id=0, has_side_effects=True, vmem_limit_bytes=56 * 1024 * 1024
        ),
    )(
        tiled(initial_state), tiled(forcing), tiled(block_inverse), tiled(lower_decay),
        tiled(upper_decay), tiled(cross_coupling), tiled(iblank),
        donor_receiver, donor_block, stencil_offset.reshape(1, senders), stencil_weight,
        fringe_target.reshape(1, slots),
    )
    return untiled(final), untiled(update)


def solution(mesh):
    return jax.shard_map(
        shards,
        mesh=mesh,
        in_specs=(
            P(None, "stream", "cross"),
            P(None, "stream", "cross"),
            P(None, None, "stream", "cross"),
            P(None, "stream", "cross"),
            P(None, "stream", "cross"),
            P("stream", "cross"),
            P("stream", "cross"),
            P(("stream", "cross"), None),
            P(("stream", "cross")),
            P(("stream", "cross")),
            P(("stream", "cross"), None),
            P(("stream", "cross")),
        ),
        out_specs=(P(None, "stream", "cross"), P(None, "stream", "cross")),
        check_vma=False,
    )
```

time: 813 us -> 96.6 us (0.12)
  the two profiles are of different devices: /device:TPU:3 before, /device:TPU:0 now
where the time goes in v1:
time: 96.6 us; the launch traced here: 96.4 us
  Pallas kernels  90.8 us (94%)
  local copies, waits for them, and re-layouts  4.96 us (5%)
    pallas_call x1, Pallas kernels, shards(): pl.pallas_call(functools.partial(kernel, ns, nc, planes, tiles), out_shap...  90.8 us
    unnamed x5, local copies, waits for them, and re-layouts  4.96 us

profile of v1, /device:TPU:0, one launch (start us, length us, event | category | flops | bytes accessed | tf_op | source)
XLA Modules:
  0.0 96.4 jit_solution(16613024689941188572)
XLA Ops:
  0.6 1.3 %copy.14.receiver_r = s32[32,1]{1,0:T(8,128)} copy(s32[32,1]{0,1:T(1,128)} %param.19) | data formatting | bytes 256 | tf_op args[7]
  2.0 90.8 %shard_map.131 = (f32[5,64,8,128]{3,2,1,0:T(8,128)}, f32[5,64,8,128]{3,2,1,0:T(8,128)}) custom-call(f32[5,64,8,128]{3,2,1,0:T(8,128)} %bitcast.30, f32[5,64,8,128]{3,2,1,0:T(8,128)} %bitcast.31, f32[5,5,64,8,128]{4,3,2,1,0:T(8,128)} %bitcast.29, f32[5,64,8,128]{3,2,1,0:T(8,128)} %bitcast.32, f32[5,64,8,128]{3,2,1,0:T(8,128)} %bitcast.33, ...), custom_call_target="tpu_custom_call" | custom-call | tf_op jit(solution)/shard_map/pallas_call | solution.py:429
  92.8 0.0 copy-start
  92.8 2.6 %copy.17 = f32[5,8,8192]{2,1,0:T(8,128)} copy(f32[5,8,8192]{2,1,0:T(8,128)} %bitcast.35) | data formatting | bytes 2621440
  95.4 0.0 copy-done
  95.4 1.1 %copy.18 = f32[5,8,8192]{2,1,0:T(8,128)} copy(f32[5,8,8192]{2,1,0:T(8,128)S(1)} %bitcast.34) | data formatting | bytes 2621440
Async XLA Ops:
  92.8 2.6 %copy-start = (f32[5,64,8,128]{3,2,1,0:T(8,128)S(1)}, f32[5,64,8,128]{3,2,1,0:T(8,128)}, u32[]{:S(2)}) copy-start(f32[5,64,8,128]{3,2,1,0:T(8,128)} %get-tuple-element.5) | copy-start | bytes 3932164

commit v2 on v1

--- a/solution.py
+++ b/solution.py
@@ -93,8 +93,8 @@
     lax.fori_loop(1, devices, greet, 0)
 
     eye = iota((senders, senders), 0) == iota((senders, senders), 1)
-    recv_col = receiver_r[...].astype(jnp.float32)
-    recv_row = jnp.sum(jnp.where(eye, recv_col, 0.0), axis=0, keepdims=True)
+    recv_row = receiver_r[...].astype(jnp.float32)
+    recv_col = jnp.sum(jnp.where(eye, recv_row, 0.0), axis=1, keepdims=True)
     earlier = iota((senders, senders), 0) < iota((senders, senders), 1)
     rank_row = jnp.sum(
         jnp.where(earlier & (recv_col == recv_row), 1.0, 0.0), axis=0, keepdims=True
@@ -466,7 +466,7 @@
     )(
         tiled(initial_state), tiled(forcing), tiled(block_inverse), tiled(lower_decay),
         tiled(upper_decay), tiled(cross_coupling), tiled(iblank),
-        donor_receiver, donor_block, stencil_offset.reshape(1, senders), stencil_weight,
+        donor_receiver.reshape(1, senders), donor_block, stencil_offset.reshape(1, senders), stencil_weight,
         fringe_target.reshape(1, slots),
     )
     return untiled(final), untiled(update)

time: 96.6 us -> 95.3 us (0.987)
  local copies, waits for them, and re-layouts: 4.96 us -> 3.62 us
    unnamed x5 -> x4, local copies, waits for them, and re-layouts: 4.96 us -> 3.62 us
where the time goes in v2:
time: 95.3 us; the launch traced here: 95.1 us
  Pallas kernels  90.8 us (95%)
  local copies, waits for them, and re-layouts  3.62 us (4%)
    pallas_call x1, Pallas kernels, shards(): pl.pallas_call(functools.partial(kernel, ns, nc, planes, tiles), out_shap...  90.8 us
    unnamed x4, local copies, waits for them, and re-layouts  3.62 us

profile of v2, /device:TPU:0, one launch (start us, length us, event | category | flops | bytes accessed | tf_op | source)
XLA Modules:
  0.0 95.1 jit_solution(903783582264383177)
XLA Ops:
  0.6 90.8 %shard_map.131 = (f32[5,64,8,128]{3,2,1,0:T(8,128)}, f32[5,64,8,128]{3,2,1,0:T(8,128)}) custom-call(f32[5,64,8,128]{3,2,1,0:T(8,128)} %bitcast.31, f32[5,64,8,128]{3,2,1,0:T(8,128)} %bitcast.32, f32[5,5,64,8,128]{4,3,2,1,0:T(8,128)} %bitcast.30, f32[5,64,8,128]{3,2,1,0:T(8,128)} %bitcast.33, f32[5,64,8,128]{3,2,1,0:T(8,128)} %bitcast.34, ...), custom_call_target="tpu_custom_call" | custom-call | tf_op jit(solution)/shard_map/pallas_call | solution.py:429
  91.5 0.0 copy-start
  91.5 2.6 %copy.16 = f32[5,8,8192]{2,1,0:T(8,128)} copy(f32[5,8,8192]{2,1,0:T(8,128)} %bitcast.36) | data formatting | bytes 2621440
  94.0 0.0 copy-done
  94.0 1.1 %copy.17 = f32[5,8,8192]{2,1,0:T(8,128)} copy(f32[5,8,8192]{2,1,0:T(8,128)S(1)} %bitcast.35) | data formatting | bytes 2621440
Async XLA Ops:
  91.5 2.6 %copy-start = (f32[5,64,8,128]{3,2,1,0:T(8,128)S(1)}, f32[5,64,8,128]{3,2,1,0:T(8,128)}, u32[]{:S(2)}) copy-start(f32[5,64,8,128]{3,2,1,0:T(8,128)} %get-tuple-element.5) | copy-start | bytes 3932164
